TPU v7x, 256 devices: a whole 4x4x8 slice. The times are simulated.
256 devices in a mesh: wide: 32 (over y, z), narrow: 8 (over x, core).
Axes of the slice: x: 4, y: 4, z: 8, core: 2. Of those that a mesh axis runs over, the one named last changes fastest.
Arguments:
- point_feats: bfloat16 [64, 524288], P(None, ('wide', 'narrow')), may hold values from -6 to 6
- edge_offset: float32 [3, 8388608], P(None, ('wide', 'narrow')), may hold values from -1.5 to 1.5
- edge_point: int32 [65536, 128], P(('wide', 'narrow')), may hold values from 0 to 2047
- block_fill: int32 [65536], P(('wide', 'narrow')), may hold values from 1 to 128, as said below
- block_owner: int32 [65536, 1], P(('wide', 'narrow')), may hold values from 0 to 31; in each aligned block of 256 rows (0 to 255, 256 to 511, ...) at most 16 rows name the same one
- block_cell: int32 [65536], P(('wide', 'narrow')), may hold values from 0 to 8191
- enc_in_w: bfloat16 [128, 6], replicated, may hold values from -2.5 to 2.5
- enc_in_b: float32 [128], replicated, may hold values from -3 to 3
- enc_mid_w: bfloat16 [128, 128], replicated, may hold values from -0.5 to 0.5
- enc_mid_b: float32 [128], replicated, may hold values from -3 to 3
- enc_out_w: bfloat16 [64, 128], replicated, may hold values from -0.5 to 0.5
- point_proj: bfloat16 [64, 64], replicated, may hold values from -0.75 to 0.75
- dec_in_w: bfloat16 [128, 6], replicated, may hold values from -2.5 to 2.5
- dec_in_b: float32 [128], replicated, may hold values from -3 to 3
- dec_mid_w: bfloat16 [128, 128], replicated, may hold values from -0.5 to 0.5
- dec_mid_b: float32 [128], replicated, may hold values from -3 to 3
- dec_out_w: bfloat16 [64, 128], replicated, may hold values from -0.5 to 0.5
- cell_proj: bfloat16 [64, 64], replicated, may hold values from -0.75 to 0.75
- skip_weight: float32 [64, 64], replicated, may hold values from -0.75 to 0.75
- skip_bias: float32 [64], replicated, may hold values from -3 to 3
- spectral_weight: float32 [32, 32, 32, 64, 128], P('wide', None, 'narrow'), may hold values from -0.5 to 0.5
Outputs:
- decoded: bfloat16 [64, 524288], P(None, ('wide', 'narrow'))
Inputs may be any that keep to these rules, and one draw needn't show every extreme that they name: `edge_point`: rows of a block name points of the device that holds the block. Rows r >= block_fill of a block are padding; every device holds a block with all 128 rows live. `block_owner`: the owner's narrow index is that of the device holding the block; among the 256 blocks of one device no wide index appears more than 16 times. `block_cell`: cell index within the owner's pencil of 4 x 128 / 8 x 128 cells, row-major.
All inputs are finite; a program needn't handle non-finite values.
Results may differ from a plain program's by a relative error of at most 0.0051.
Values may be sent and summed in bfloat16 or wider, within the bound.
A program may use at most 128 MiB of HBM per device.

v0:
```python
import math

import jax
import jax.numpy as jnp
from jax import lax
from jax.sharding import PartitionSpec as P

G = 128
M = 32


highest = lax.Precision.HIGHEST


def tables(length, number):
    position = jnp.arange(length, dtype=jnp.int32)
    waves = jnp.arange(number, dtype=jnp.int32) - number // 2
    phases = position[:, None] * waves[None, :] % length
    angles = phases.astype(jnp.float32) * (2.0 * math.pi / length)
    return (jnp.cos(angles), jnp.sin(angles))


def kernel(first_w, first_b, second_w, second_b, third_w, features):
    hidden = jax.nn.gelu(
        jnp.dot(first_w, features, preferred_element_type=jnp.float32) + first_b[:, None]
    ).astype(jnp.bfloat16)
    hidden = jax.nn.gelu(
        jnp.dot(second_w, hidden, preferred_element_type=jnp.float32) + second_b[:, None]
    ).astype(jnp.bfloat16)
    return jnp.dot(third_w, hidden, preferred_element_type=jnp.float32)


def einsum_high(form, left, right):
    return jnp.einsum(form, left, right, precision=highest)


def shards(
    point_feats,
    edge_offset,
    edge_point,
    block_fill,
    block_owner,
    block_cell,
    enc_in_w,
    enc_in_b,
    enc_mid_w,
    enc_mid_b,
    enc_out_w,
    point_proj,
    dec_in_w,
    dec_in_b,
    dec_mid_w,
    dec_mid_b,
    dec_out_w,
    cell_proj,
    skip_weight,
    skip_bias,
    spectral_weight,
):
    wide_count = lax.axis_size("wide")
    narrow_count = lax.axis_size("narrow")
    chans = point_feats.shape[0]
    point_count = point_feats.shape[1]
    blocks, rows_per = edge_point.shape
    x_local = G // wide_count
    y_local = G // narrow_count
    cells_here = x_local * y_local * G
    slots = 2 * blocks // wide_count
    wide_here = lax.axis_index("wide")
    narrow_here = lax.axis_index("narrow")
    owners = block_owner[:, 0]
    coord_x = owners * x_local + block_cell // (y_local * G)
    coord_y = narrow_here * y_local + block_cell // G % y_local
    coord_z = block_cell % G
    centres = (
        2.0 * jnp.stack([coord_x, coord_y, coord_z], axis=0).astype(jnp.float32) + 1.0
    ) / G - 1.0
    live = (jnp.arange(rows_per, dtype=jnp.int32)[None, :] < block_fill[:, None]).reshape(-1)
    flat_points = edge_point.reshape(-1)
    features = jnp.concatenate([edge_offset, jnp.repeat(centres, rows_per, axis=1)], axis=0).astype(
        jnp.bfloat16
    )
    enc_kernel = kernel(enc_in_w, enc_in_b, enc_mid_w, enc_mid_b, enc_out_w, features)
    projected = jnp.dot(point_proj, point_feats, preferred_element_type=jnp.float32).astype(
        jnp.bfloat16
    )
    picked = jnp.take(projected, flat_points, axis=1).astype(jnp.float32)
    message = jnp.where(live[None, :], enc_kernel * picked, 0.0)
    block_sums = message.reshape(chans, blocks, rows_per).sum(axis=2)
    onehot = (owners[:, None] == jnp.arange(wide_count, dtype=jnp.int32)[None, :]).astype(jnp.int32)
    earlier = jnp.cumsum(onehot, axis=0) - onehot
    target = owners * slots + jnp.sum(earlier * onehot, axis=1)
    placer = (target[None, :] == jnp.arange(wide_count * slots, dtype=jnp.int32)[:, None]).astype(
        jnp.float32
    )
    send_sums = jnp.dot(placer, block_sums.T, precision=highest).reshape(wide_count, slots * chans)
    send_counts = jnp.dot(placer, block_fill.astype(jnp.float32), precision=highest).reshape(
        wide_count, slots
    )
    send_cells = jnp.dot(placer, block_cell.astype(jnp.float32), precision=highest).reshape(
        wide_count, slots
    )
    recv_sums, recv_counts, recv_cells = (
        lax.all_to_all(send_sums, "wide", split_axis=0, concat_axis=0, tiled=True),
        lax.all_to_all(send_counts, "wide", split_axis=0, concat_axis=0, tiled=True),
        lax.all_to_all(send_cells, "wide", split_axis=0, concat_axis=0, tiled=True),
    )
    cell_index = recv_cells.reshape(-1).astype(jnp.int32)
    entry_sums = recv_sums.reshape(-1, chans)
    totals = jnp.zeros((chans, cells_here), jnp.float32).at[:, cell_index].add(entry_sums.T)
    counts = jnp.zeros((cells_here,), jnp.float32).at[cell_index].add(recv_counts.reshape(-1))
    scales = jnp.maximum(jnp.sqrt(counts), 1.0)
    latent = (totals / scales[None, :]).reshape(chans, x_local, y_local, G)
    dec_kernel = kernel(dec_in_w, dec_in_b, dec_mid_w, dec_mid_b, dec_out_w, features)
    cos_t, sin_t = tables(G, M)
    cos_rows = lax.dynamic_slice_in_dim(cos_t, wide_here * x_local, x_local, 0)
    sin_rows = lax.dynamic_slice_in_dim(sin_t, wide_here * x_local, x_local, 0)
    real_z = einsum_high("cxyz,zk->xykc", latent, cos_t)
    imag_z = -einsum_high("cxyz,zk->xykc", latent, sin_t)
    columns = lax.all_to_all(
        jnp.concatenate([real_z, imag_z], axis=3), "narrow", split_axis=2, concat_axis=1, tiled=True
    )
    real_part = columns[..., :chans]
    imag_part = columns[..., chans:]
    real_y = einsum_high("xykc,yj->xjkc", real_part, cos_t) + einsum_high(
        "xykc,yj->xjkc", imag_part, sin_t
    )
    imag_y = einsum_high("xykc,yj->xjkc", imag_part, cos_t) - einsum_high(
        "xykc,yj->xjkc", real_part, sin_t
    )
    y_modes = jnp.concatenate([real_y, imag_y], axis=3)
    piece = y_modes
    real_piece = piece[..., :chans]
    imag_piece = piece[..., chans:]
    real_out = einsum_high("xjkc,xi->jikc", real_piece, cos_rows) + einsum_high(
        "xjkc,xi->jikc", imag_piece, sin_rows
    )
    imag_out = einsum_high("xjkc,xi->jikc", imag_piece, cos_rows) - einsum_high(
        "xjkc,xi->jikc", real_piece, sin_rows
    )
    x_modes = lax.psum_scatter(
        jnp.concatenate([real_out, imag_out], axis=3), "wide", scatter_dimension=0, tiled=True
    )
    real_in = x_modes[..., :chans]
    imag_in = x_modes[..., chans:]
    real_mix = einsum_high("jikc,jikcd->jikd", real_in, spectral_weight)
    imag_mix = einsum_high("jikc,jikcd->jikd", imag_in, spectral_weight)
    mixed_modes = jnp.concatenate(
        [
            real_mix[..., :chans] - imag_mix[..., chans:],
            real_mix[..., chans:] + imag_mix[..., :chans],
        ],
        axis=3,
    )
    piece = lax.all_gather(mixed_modes, "wide", axis=0, tiled=True)
    real_piece = piece[..., :chans]
    imag_piece = piece[..., chans:]
    real_back = einsum_high("jikc,xi->xjkc", real_piece, cos_rows) - einsum_high(
        "jikc,xi->xjkc", imag_piece, sin_rows
    )
    imag_back = einsum_high("jikc,xi->xjkc", imag_piece, cos_rows) + einsum_high(
        "jikc,xi->xjkc", real_piece, sin_rows
    )
    back_modes = jnp.concatenate([real_back, imag_back], axis=3)
    real_back_y = back_modes[..., :chans]
    imag_back_y = back_modes[..., chans:]
    grid_real = einsum_high("xjkc,yj->xykc", real_back_y, cos_t) - einsum_high(
        "xjkc,yj->xykc", imag_back_y, sin_t
    )
    grid_imag = einsum_high("xjkc,yj->xykc", imag_back_y, cos_t) + einsum_high(
        "xjkc,yj->xykc", real_back_y, sin_t
    )
    slabs = lax.all_to_all(
        jnp.concatenate([grid_real, grid_imag], axis=3),
        "narrow",
        split_axis=1,
        concat_axis=2,
        tiled=True,
    )
    slab_real = slabs[..., :chans]
    slab_imag = slabs[..., chans:]
    spectral = (
        einsum_high("xykc,zk->cxyz", slab_real, cos_t)
        - einsum_high("xykc,zk->cxyz", slab_imag, sin_t)
    ) / (M * M * M)
    linear = einsum_high("cxyz,cd->dxyz", latent, skip_weight) + skip_bias[:, None, None, None]
    field = jax.nn.gelu(spectral + linear).astype(jnp.bfloat16).reshape(chans, cells_here)
    reply = jnp.take(field, cell_index, axis=1).T.reshape(wide_count, slots * chans)
    returned = lax.all_to_all(reply, "wide", split_axis=0, concat_axis=0, tiled=True).reshape(
        wide_count * slots, chans
    )
    values = jnp.take(returned, target, axis=0)
    gathered = jnp.dot(cell_proj, values.T, preferred_element_type=jnp.float32)
    dec_message = jnp.where(live[None, :], dec_kernel * jnp.repeat(gathered, rows_per, axis=1), 0.0)
    point_sums = jnp.zeros((chans, point_count), jnp.float32).at[:, flat_points].add(dec_message)
    degree = jnp.zeros((point_count,), jnp.float32).at[flat_points].add(live.astype(jnp.float32))
    return (point_sums / jnp.maximum(jnp.sqrt(degree), 1.0)[None, :]).astype(jnp.bfloat16)


def solution(mesh):
    return jax.shard_map(
        shards,
        mesh=mesh,
        in_specs=(
            P(None, ("wide", "narrow")),
            P(None, ("wide", "narrow")),
            P(("wide", "narrow"), None),
            P(("wide", "narrow")),
            P(("wide", "narrow"), None),
            P(("wide", "narrow")),
            P(),
            P(),
            P(),
            P(),
            P(),
            P(),
            P(),
            P(),
            P(),
            P(),
            P(),
            P(),
            P(),
            P(),
            P("wide", None, "narrow", None, None),
        ),
        out_specs=P(None, ("wide", "narrow")),
        check_vma=False,
    )
```

profile of v0, /device:TPU:1, one launch (start us, length us, event | category | flops | bytes accessed | tf_op | source)
XLA Modules:
  0.0 1019.1 jit_solution(12288276415593771673)
XLA Ops:
  10.7 12.0 %all-to-all-start = ((f32[32,1,16]{2,1,0:T(1,128)}), f32[32,1,16]{2,1,0:T(1,128)S(1)}, u32[]{:S(2)}, u32[]{:S(2)}) async-start(f32[32,1,16]{2,1,0:T(1,128)} %bitcast.10), calls=%async_computation | async-start | bytes 32768 | tf_op jit(solution)/shard_map/all_to_all | solution.py:106
  26.6 1.1 convert.8
  28.9 114.2 %gather_fusion = bf16[32768,64]{1,0:T(8,128)(2,1)} fusion(bf16[64,2048]{0,1:T(8,128)(2,1)S(1)} %copy.177, s32[32768]{0:T(1024)S(1)} %broadcast_clamp_fusion), kind=kCustom, calls=%fused_computation | custom fusion | bytes 8519680 | tf_op jit(solution)/shard_map/jit(_take)/gather | solution.py:87
  143.1 8.6 copy.178
  151.8 14.3 %fusion.39 = bf16[128,32768]{0,1:T(8,128)(2,1)} fusion(bf16[128,128]{1,0:T(8,128)(2,1)S(1)} %copy-done.12, bf16[128,6]{0,1:T(8,128)(2,1)S(1)} %copy-done.14, f32[128]{0:T(128)S(1)} %copy-done.16, f32[128]{0:T(128)S(1)} %copy-done.17, bf16[3,32768]{1,0:T(4,128)(2,1)S(1)} %bitcast.241, bf16[3,32768]{1,0:T(4,128)(2,1)S(1)} %convert.8), kind=kOutput, calls=%fused_computation.56 | convolution fusion | flops 1208745984 | bytes 8817152 | tf_op jit(solution)/shard_map/dot_general | solution.py:28
  166.1 7.6 fusion.54
  173.7 1.5 copy.250
  175.1 2.2 bitcast_reduce_fusion
  178.8 9.2 all-to-all-start.2
  189.0 7.7 all-to-all-done.2
  196.6 4.1 all-to-all-start.1
  202.2 3.3 scatter_custom_fusion.1
  205.5 4.5 all-to-all-done.1
  210.4 4.4 scatter_custom_fusion
  214.8 5.0 broadcast_divide_fusion
  219.8 2.4 fusion.73
  222.2 2.4 convolution_bitcast_fusion.1
  224.9 1.6 copy.184
  226.5 8.1 all-to-all-start.3
  234.7 9.4 reduce-scatter.2.cloned.1.call-start
  244.2 5.5 all-to-all-done.3
  253.3 1.8 fusion.108
  255.1 1.8 fusion.112
  256.9 2.0 subtract_bitcast_fusion
  258.9 2.0 add_bitcast_fusion
  260.9 2.0 pad_maximum_fusion
  263.0 205.7 %reduce-scatter.2.cloned.1.call-done = f32[1,32,4,128]{3,1,2,0:T(8,128)} async-done(((f32[32,32,4,128]{3,1,2,0:T(8,128)}), f32[1,32,4,128]{3,1,2,0:T(8,128)}) %reduce-scatter.2.cloned.1.call-update) | async-done | bytes 65552 | tf_op jit(solution)/shard_map/reduce_scatter | solution.py:141
  469.7 5.3 fusion.52
  475.0 5.7 fusion.50
  481.6 77.7 %all-gather.2.cloned.1.call-done = f32[32,32,4,128]{3,1,2,0:T(8,128)} async-done(((f32[1,32,4,128]{3,1,2,0:T(8,128)}), f32[32,32,4,128]{3,1,2,0:T(8,128)}) %all-gather.2.cloned.1.call-update) | async-done | bytes 2097168 | tf_op jit(solution)/shard_map/all_gather | solution.py:155
  559.2 3.2 fusion.67
  562.4 2.8 fusion.78
  566.3 3.1 fusion.65
  569.4 1.2 fusion.81
  573.9 1.5 copy.205
  575.3 9.0 all-to-all-start.4
  584.4 14.3 %fusion.23 = bf16[128,32768]{0,1:T(8,128)(2,1)} fusion(bf16[128,128]{1,0:T(8,128)(2,1)S(1)} %copy-done.13, bf16[128,6]{0,1:T(8,128)(2,1)S(1)} %copy-done.15, f32[128]{0:T(128)S(1)} %copy-done.18, f32[128]{0:T(128)S(1)} %copy-done.19, bf16[3,32768]{1,0:T(4,128)(2,1)S(1)} %bitcast.242, bf16[3,32768]{1,0:T(4,128)(2,1)S(1)} %convert.8), kind=kOutput, calls=%fused_computation.40 | convolution fusion | flops 1208745984 | bytes 8817152 | tf_op jit(solution)/shard_map/dot_general | solution.py:28
  598.7 172.8 %scatter_custom_fusion.3 = f32[2048]{0:T(1024)S(1)} fusion(s32[32768]{0:T(1024)S(1)} %bitcast.239, f32[32768]{0:T(1024)S(1)} %get-tuple-element.11, f32[]{:T(128)} %constant.127.clone.1), kind=kCustom, calls=%fused_computation.232 | custom fusion | flops 32768 | bytes 8196 | tf_op jit(solution)/shard_map/scatter-add | solution.py:196
  773.2 3.8 fusion.84
  777.0 3.5 fusion.86
  780.6 5.7 fusion.62
  787.4 1.3 gather_fusion.1
  791.8 5.3 all-to-all-start.5
  797.2 8.8 all-to-all-done.5
  808.4 2.3 broadcast_in_dim.94
  810.7 13.4 %fusion.7 = f32[32768,64]{0,1:T(8,128)} fusion(bf16[128,32768]{0,1:T(8,128)(2,1)} %fusion.23, bf16[64,128]{1,0:T(8,128)(2,1)S(1)} %copy-done.9, f32[8,8,256,128]{3,2,1,0:T(8,128)S(1)} %bitcast.227, pred[32768]{0:T(1024)(128)(4,1)S(1)} %copy-done.6), kind=kOutput, calls=%fused_computation.20 | convolution fusion | flops 541065216 | bytes 25214976 | tf_op jit(solution)/shard_map/dot_general | solution.py:30
  824.1 12.2 %copy.213 = f32[32768,64]{1,0:T(8,128)} copy(f32[32768,64]{0,1:T(8,128)} %fusion.7) | data formatting | bytes 16777216 | tf_op jit(solution)/shard_map/jit(_where)/select_n | solution.py:194
  836.3 174.5 %scatter_custom_fusion.2 = f32[64,2048]{0,1:T(8,128)S(1)} fusion(s32[32768]{0:T(1024)S(1)} %bitcast.240, f32[32768,64]{1,0:T(8,128)} %copy.213, f32[]{:T(128)} %constant.127.clone.1), kind=kCustom, calls=%fused_computation.131 | custom fusion | flops 2097152 | bytes 524800 | tf_op jit(solution)/shard_map/scatter-add | solution.py:195
  (116 shorter events, 32.8 us)
Async XLA Ops:
  6.5 21.2 %copy-start = (bf16[64,2048]{1,0:T(8,128)(2,1)S(1)}, bf16[64,2048]{1,0:T(8,128)(2,1)}, u32[]{:S(2)}) copy-start(bf16[64,2048]{1,0:T(8,128)(2,1)} %param.21) | copy-start | bytes 786436
  10.7 168.1 %all-to-all-start = ((f32[32,1,16]{2,1,0:T(1,128)}), f32[32,1,16]{2,1,0:T(1,128)S(1)}, u32[]{:S(2)}, u32[]{:S(2)}) async-start(f32[32,1,16]{2,1,0:T(1,128)} %bitcast.10), calls=%async_computation | async-start | bytes 32768 | tf_op jit(solution)/shard_map/all_to_all | solution.py:106
  24.2 141.9 %copy-start.5 = (pred[32768]{0:T(1024)(128)(4,1)}, pred[32768]{0:T(1024)(128)(4,1)S(1)}, u32[]{:S(2)}) copy-start(pred[32768]{0:T(1024)(128)(4,1)S(1)} %get-tuple-element.12) | copy-start | bytes 98308
  143.1 8.6 copy-start.12
  143.1 8.6 copy-start.14
  143.1 8.6 copy-start.16
  143.1 8.6 copy-start.17
  151.8 14.3 %copy-start.8 = (bf16[64,128]{1,0:T(8,128)(2,1)S(1)}, bf16[64,128]{1,0:T(8,128)(2,1)}, u32[]{:S(2)}) copy-start(bf16[64,128]{1,0:T(8,128)(2,1)} %param.31) | copy-start | bytes 49156
  178.8 17.9 %all-to-all-start.2 = ((f32[32,1,16]{2,1,0:T(1,128)}), f32[32,1,16]{2,1,0:T(1,128)S(1)}, u32[]{:S(2)}, u32[]{:S(2)}) async-start(f32[32,1,16]{2,1,0:T(1,128)} %bitcast.24), calls=%async_computation.2 | async-start | bytes 32768 | tf_op jit(solution)/shard_map/all_to_all | solution.py:105
  196.6 13.4 %all-to-all-start.1 = ((f32[32,1,1024]{2,1,0:T(1,128)}), f32[32,1,1024]{2,1,0:T(1,128)S(1)}, u32[]{:S(2)}, u32[]{:S(2)}) async-start(f32[32,1,1024]{2,1,0:T(1,128)} %all_to_all.66), calls=%async_computation.1 | async-start | bytes 262144 | tf_op jit(solution)/shard_map/all_to_all | solution.py:104
  219.8 2.4 copy-start.2
  226.5 23.2 %all-to-all-start.3 = ((f32[4,16,32,128]{3,1,0,2:T(8,128)}), f32[4,16,32,128]{3,1,0,2:T(8,128)S(1)}, u32[]{:S(2)}, u32[]{:S(2)}) async-start(f32[4,16,32,128]{3,1,0,2:T(8,128)} %copy.184), calls=%async_computation.3 | async-start | bytes 2097152 | tf_op jit(solution)/shard_map/all_to_all | solution.py:120
  234.7 234.0 %reduce-scatter.2.cloned.1.call-start = ((), (), s32[]{:S(2)}) async-start(), calls=%async_computation.7 | async-start | bytes 2162688 | tf_op jit(solution)/shard_map/reduce_scatter | solution.py:141
  262.9 296.3 %all-gather.2.cloned.1.call-start = ((), (), s32[]{:S(2)}) async-start(), calls=%async_computation.8 | async-start | bytes 2162688 | tf_op jit(solution)/shard_map/all_gather | solution.py:155
  559.2 10.2 copy-start.4
  565.2 19.1 %copy-start.13 = (bf16[128,128]{1,0:T(8,128)(2,1)S(1)}, bf16[128,128]{1,0:T(8,128)(2,1)}, u32[]{:S(2)}) copy-start(bf16[128,128]{1,0:T(8,128)(2,1)} %param.35) | copy-start | bytes 98308
  565.2 19.1 %copy-start.15 = (bf16[128,6]{0,1:T(8,128)(2,1)S(1)}, bf16[128,6]{0,1:T(8,128)(2,1)}, u32[]{:S(2)}) copy-start(bf16[128,6]{0,1:T(8,128)(2,1)} %param.33) | copy-start | bytes 4612
  565.2 19.1 %copy-start.18 = (f32[128]{0:T(128)S(1)}, f32[128]{0:T(128)}, u32[]{:S(2)}) copy-start(f32[128]{0:T(128)} %param.36) | copy-start | bytes 1540
  565.2 19.1 %copy-start.19 = (f32[128]{0:T(128)S(1)}, f32[128]{0:T(128)}, u32[]{:S(2)}) copy-start(f32[128]{0:T(128)} %param.34) | copy-start | bytes 1540
  575.3 196.9 %all-to-all-start.4 = ((f32[4,128,4,128]{3,2,0,1:T(4,128)}), f32[4,128,4,128]{3,2,0,1:T(4,128)S(1)}, u32[]{:S(2)}, u32[]{:S(2)}) async-start(f32[4,128,4,128]{3,2,0,1:T(4,128)} %copy.205), calls=%async_computation.5 | async-start | bytes 2097152 | tf_op jit(solution)/shard_map/all_to_all | solution.py:173
  598.7 181.9 %copy-start.7 = (f32[64,64]{1,0:T(8,128)S(1)}, f32[64,64]{1,0:T(8,128)}, u32[]{:S(2)}) copy-start(f32[64,64]{1,0:T(8,128)} %param.39) | copy-start | bytes 49156
  598.7 181.9 %copy-start.11 = (f32[64]{0:T(128)S(1)}, f32[64]{0:T(128)}, u32[]{:S(2)}) copy-start(f32[64]{0:T(128)} %param.40) | copy-start | bytes 772
  772.2 8.4 copy-start.3
  777.0 20.1 %copy-start.10 = (s32[256,1]{0,1:T(1,128)S(1)}, s32[256,1]{0,1:T(1,128)}, u32[]{:S(2)}) copy-start(s32[256,1]{0,1:T(1,128)} %param.25) | copy-start | bytes 3076
  787.3 23.3 %copy-start.6 = (pred[32768]{0:T(1024)(128)(4,1)S(1)}, pred[32768]{0:T(1024)(128)(4,1)}, u32[]{:S(2)}) copy-start(pred[32768]{0:T(1024)(128)(4,1)} %copy-done.5) | copy-start | bytes 98308
  787.4 23.3 %copy-start.9 = (bf16[64,128]{1,0:T(8,128)(2,1)S(1)}, bf16[64,128]{1,0:T(8,128)(2,1)}, u32[]{:S(2)}) copy-start(bf16[64,128]{1,0:T(8,128)(2,1)} %param.37) | copy-start | bytes 49156
  791.8 14.2 %all-to-all-start.5 = ((bf16[32,2,512]{2,1,0:T(2,128)(2,1)}), bf16[32,2,512]{2,1,0:T(2,128)(2,1)S(1)}, u32[]{:S(2)}, u32[]{:S(2)}) async-start(bf16[32,2,512]{2,1,0:T(2,128)(2,1)} %reshape.304), calls=%async_computation.6 | async-start | bytes 131072 | tf_op jit(solution)/shard_map/all_to_all | solution.py:189
  810.7 201.2 %copy-start.1 = (bf16[64,2048]{1,0:T(8,128)(2,1)S(1)}, bf16[64,2048]{1,0:T(8,128)(2,1)}, u32[]{:S(2)}) copy-start(bf16[64,2048]{1,0:T(8,128)(2,1)} %param.21) | copy-start | bytes 786436
Sparse Core Ops, SparseCore 0:
  263.1 205.5 reduce-scatter.1
  481.7 77.4 all-gather.1
where the time goes:
time: 1030 us; the launch traced here: 1020 us
  other arithmetic  378 us (37%)
  waiting for transfers between devices  310 us (30%)
  local copies, waits for them, and re-layouts  153 us (15%)
  matrix products  107 us (10%)
  starting transfers between devices  57.2 us (6%)
  between operations  14.5 us (1%)
    reduce_scatter x1, waiting for transfers between devices, shards(): lax.psum_scatter(jnp.concatenate([real_out, imag_out], axis=3), 'wide', s...  206 us
    scatter-add x1, other arithmetic, shards(): jnp.zeros((chans, point_count), jnp.float32).at[:, flat_points]  174 us
    scatter-add x1, other arithmetic, shards(): jnp.zeros((point_count,), jnp.float32).at[flat_points]  173 us
    gather x2, local copies, waits for them, and re-layouts, shards(): picked = jnp.take(projected, flat_points, axis=1).astype(jnp.float32)  123 us
    all_gather x1, waiting for transfers between devices, shards(): piece = lax.all_gather(mixed_modes, 'wide', axis=0, tiled=True)  77.7 us
    dot_general x23, matrix products, einsum_high(): return jnp.einsum(form, left, right, precision=highest)  54.2 us
    dot_general x2, matrix products, kernel(): jnp.dot(second_w, hidden, preferred_element_type=jnp.float32)  28.6 us
    dot_general x2, matrix products, kernel(): return jnp.dot(third_w, hidden, preferred_element_type=jnp.float32)  21 us
  transfers between devices with their start and end apart: 8, of which 6 were waited for; matrix products, arithmetic and copies ran while one was open for 34% of the time, Pallas kernels for 0%

commit v1 on v0

v1 whole, which is shorter than its diff:
```python
import functools
import math

import jax
import jax.numpy as jnp
import numpy as np
from jax import lax
from jax.experimental import pallas as pl
from jax.experimental.pallas import tpu as pltpu
from jax.sharding import PartitionSpec as P

G = 128
M = 32
C = 64
H = 128
ROWS = 128
WIDE = 32
NARROW = 8
SLOTS = 16
ENTRIES = WIDE * SLOTS
XL = G // WIDE
YL = G // NARROW
KZ = M // NARROW
PTS = 2048
BLKS = 256
LOW = 256
HIGH = PTS // LOW
STEP_BLKS = 16
LANES = STEP_BLKS * ROWS
SUB = 256
BF = jnp.bfloat16
F32 = jnp.float32

NT = (((1,), (1,)), ((), ()))
TN = (((0,), (0,)), ((), ()))


def dot(left, right, dims=(((1,), (0,)), ((), ()))):
    return lax.dot_general(left, right, dims, preferred_element_type=F32)


def angles(positions, waves):
    return 2.0 * np.pi * (np.outer(positions, waves) % G) / G


WAVES = np.arange(M) - M // 2


def z_table():
    turn = angles(np.arange(G), WAVES)
    both = np.stack([np.cos(turn), -np.sin(turn)], axis=2)
    return np.repeat(both.reshape(G, 2 * M), C, axis=1).astype(BF)


def y_forward_table():
    turn = angles(WAVES, np.arange(G))
    return np.concatenate([np.cos(turn), np.sin(turn)], axis=0).astype(BF)


def y_inverse_table():
    turn = angles(np.arange(G), WAVES)
    return np.concatenate([np.cos(turn), np.sin(turn)], axis=0).astype(BF)


def x_forward_table():
    turn = angles(WAVES, np.arange(G))
    same = np.eye(KZ)
    halves = []
    for wave in (np.cos(turn), np.sin(turn)):
        full = np.einsum("ix,kl->ikxl", wave, same)
        full = np.repeat(full[:, None], 2, axis=1)
        halves.append(full.reshape(M * 2 * KZ, G * KZ))
    return np.concatenate(halves, axis=0).astype(BF)


def x_inverse_table():
    turn = angles(np.arange(G), WAVES)
    same = np.eye(KZ)
    cos, sin = np.cos(turn) / M**3, np.sin(turn) / M**3
    halves = []
    for first, second in ((cos, -sin), (sin, cos)):
        full = np.einsum("xis,kl->xkisl", np.stack([first, second], axis=2), same)
        halves.append(full.reshape(G * KZ, M * 2 * KZ))
    return np.concatenate(halves, axis=0).astype(BF)


def half_gelu(half):
    slope = math.sqrt(2.0 / math.pi)
    inner = half * (half * half * (8.0 * slope * 0.044715) + 2.0 * slope)
    return half + half * jnp.tanh(inner)


def turned(value):
    lane = lax.broadcasted_iota(jnp.int32, value.shape, 1)
    rolled = pltpu.roll(value, C, 1)
    return jnp.where(lane < C, -rolled, rolled)


def network(first_w, second_w, second_b, third_w, features):
    hidden = half_gelu(dot(first_w, features)).astype(BF)
    bias = jnp.concatenate([second_b] * (features.shape[1] // second_b.shape[1]), axis=1)
    hidden = half_gelu(dot(second_w, hidden) + bias).astype(BF)
    return dot(third_w, hidden)


def block_lanes():
    lane = lax.broadcasted_iota(jnp.int32, (STEP_BLKS, LANES), 1)
    return lane - lax.broadcasted_iota(jnp.int32, (STEP_BLKS, LANES), 0) * ROWS


def edge_features(offsets_ref, centres_ref, distance, features_ref):
    inside = jnp.where((distance >= 0) & (distance < ROWS), 1.0, 0.0).astype(BF)
    features_ref[...] = dot(centres_ref[0], inside)
    features_ref[0:3, :] = offsets_ref[...]
    return features_ref[...].astype(BF)


def point_rows(points_ref, sub):
    per = SUB // ROWS
    return jnp.concatenate([points_ref[sub * per + i : sub * per + i + 1, :] for i in range(per)], axis=1)


def low_onehot(row, iota_ref):
    low = jnp.broadcast_to((row & (LOW - 1)).astype(F32), (16, SUB)).astype(BF)
    low = jnp.concatenate([low] * (LOW // 16), axis=0)
    return jnp.where(low == iota_ref[...], jnp.ones((), BF), jnp.zeros((), BF))


def fill_iota(iota_ref):
    iota_ref[...] = lax.broadcasted_iota(jnp.int32, (LOW, SUB), 0).astype(F32).astype(BF)


def encode_body(
    owner_row, owner_col, meta, feats, proj, w1, w2, b2, w3, centres, fill, offsets, points,
    sent, grouped, sums, features, iota,
):
    step = pl.program_id(0)

    @pl.when(step == 0)
    def _():
        projected = dot(proj[...], feats[...]).astype(BF)
        for high in range(HIGH):
            grouped[high * C : (high + 1) * C, :] = projected[:, high * LOW : (high + 1) * LOW]
        fill_iota(iota)
        sums[...] = meta[...]

    distance = block_lanes()
    live = jnp.where((distance >= 0) & (distance < fill[...]), 1.0, 0.0).astype(BF)
    inputs = edge_features(offsets, centres, distance, features)
    messages = []
    for sub in range(LANES // SUB):
        lanes = slice(sub * SUB, (sub + 1) * SUB)
        weight = network(w1[...], w2[...], b2[...], w3[...], inputs[:, lanes])
        row = point_rows(points, sub)
        spread = dot(grouped[...], low_onehot(row, iota))
        high_row = jnp.broadcast_to(row >> 8, (C, SUB))
        picked = spread[0:C]
        for high in range(1, HIGH):
            picked = jnp.where(high_row == high, spread[high * C : (high + 1) * C], picked)
        messages.append((weight * picked).astype(BF))
    message = jnp.concatenate(messages, axis=1)
    rows = pl.ds(pl.multiple_of(step * STEP_BLKS, STEP_BLKS), STEP_BLKS)
    sums[rows, 0:C] = dot(live, message, NT)

    @pl.when(step == BLKS // STEP_BLKS - 1)
    def _():
        before = lax.broadcasted_iota(jnp.int32, (BLKS, BLKS), 0) < lax.broadcasted_iota(
            jnp.int32, (BLKS, BLKS), 1
        )
        same = owner_col[...] == owner_row[...]
        rank = jnp.sum(jnp.where(same & before, 1, 0), axis=0, keepdims=True)
        target = owner_row[...] * SLOTS + rank
        slot = lax.broadcasted_iota(jnp.int32, (ENTRIES, BLKS), 0)
        placer = jnp.where(slot == target, 1.0, 0.0).astype(BF)
        sent[...] = dot(placer, sums[...].astype(BF)).astype(BF)


def entry_cells(received):
    cell_row = received[:, C : C + 1].astype(F32)
    cell_z = received[:, C + 1 : C + 2].astype(F32)
    lane = lax.broadcasted_iota(jnp.int32, (16, 2 * C), 1)
    sub = lax.broadcasted_iota(jnp.int32, (16, 2 * C), 0)
    picker = jnp.where(lane == sub + C, 1.0, 0.0).astype(BF)
    rows = dot(picker, received, NT)
    return cell_row, cell_z, rows[0:1, :], rows[1:2, :]


def forward_z_body(received_ref, table, out, latent):
    received = received_ref[...]
    cell_row, cell_z, row_xy, row_z = entry_cells(received)
    same = (cell_row * G + cell_z) == (row_xy * G + row_z)
    totals = dot(jnp.where(same, 1.0, 0.0).astype(BF), received)
    scale = 1.0 / jnp.maximum(jnp.sqrt(totals[:, C + 2 : C + 3]), 1.0)
    latent[...] = totals * scale
    own = received.astype(F32) * scale
    lane = lax.broadcasted_iota(jnp.int32, own.shape, 1)
    own = jnp.where(lane < C, own, pltpu.roll(own, C, 1))
    position = lax.broadcasted_iota(jnp.int32, (ENTRIES, G), 1).astype(F32)
    at_z = jnp.where(position == cell_z, 1.0, 0.0).astype(BF)
    pencil = lax.broadcasted_iota(jnp.int32, (XL * YL, ENTRIES), 0).astype(F32)
    at_row = jnp.where(pencil == row_xy, 1.0, 0.0).astype(BF)
    width = KZ * 2 * C
    spread = jnp.concatenate([own] * KZ, axis=1)
    for group in range(NARROW):
        phases = dot(at_z, table[:, group * width : (group + 1) * width])
        modes = dot(at_row, (spread * phases).astype(BF)).astype(BF)
        for x in range(XL):
            out[group, :, x * width : (x + 1) * width] = modes[x * YL : (x + 1) * YL, :]


def forward_y_body(received, table, out, columns):
    both = dot(table[...], received[...])
    for j in range(XL * KZ):
        lanes = slice(j * 2 * C, (j + 1) * 2 * C)
        columns[pl.ds(j, M, stride=XL * KZ), :] = both[0:M, lanes] - turned(both[M:, lanes])
    out[...] = columns[...].astype(BF)


def x_body(received, forward, inverse, weight, out, left, product):
    count = M * 2 * KZ
    both = dot(forward[...], received[...])
    modes = both[0:count] - turned(both[count:])
    row = lax.broadcasted_iota(jnp.int32, (count, 2 * C), 0)
    lane = lax.broadcasted_iota(jnp.int32, (count, 2 * C), 1)
    real_row = (row // KZ) % 2 == 0
    wide = jnp.where(real_row == (lane < C), modes, pltpu.roll(modes, C, 1))
    for half in range(KZ // 2):
        keep = row % KZ == 2 * half + lane // C
        left[:, half * 2 * C : (half + 1) * 2 * C] = jnp.where(keep, wide, 0.0)
    for kx in range(M):
        rows = slice(kx * 2 * KZ, (kx + 1) * 2 * KZ)
        mixer = weight[kx].reshape(KZ * C, 2 * C).astype(BF)
        product[rows, :] = dot(left[rows, :].astype(BF), mixer)
    back = dot(inverse[...], product[...].astype(BF))
    cells = G * KZ
    out[...] = (back[0:cells] + turned(back[cells:])).astype(BF)


def inverse_y_body(received, table, out, columns):
    columns[...] = received[...].astype(F32)
    for j in range(XL * KZ):
        column = columns[pl.ds(j, M, stride=XL * KZ), :].astype(BF)
        both = dot(table[...], column)
        value = both[0:G] + turned(both[G:])
        out[:, j * 2 * C : (j + 1) * 2 * C] = value.astype(BF)


def inverse_z_body(received_ref, latent, spectra, table, skip, bias, out):
    received = received_ref[...]
    cell_row = received[:, C : C + 1].astype(F32)
    cell_z = received[:, C + 1 : C + 2].astype(F32)
    position = lax.broadcasted_iota(jnp.int32, (ENTRIES, G), 1).astype(F32)
    at_z = jnp.where(position == cell_z, 1.0, 0.0).astype(BF)
    pencil = lax.broadcasted_iota(jnp.int32, (ENTRIES, XL * YL), 1).astype(F32)
    at_row = jnp.where(pencil == cell_row, 1.0, 0.0).astype(BF)
    width = KZ * 2 * C
    total = jnp.zeros((ENTRIES, 2 * C), F32)
    for group in range(NARROW):
        phases = dot(at_z, table[:, group * width : (group + 1) * width])
        pencils = jnp.concatenate(
            [spectra[group, :, x * width : (x + 1) * width] for x in range(XL)], axis=0
        )
        terms = phases * dot(at_row, pencils)
        for j in range(KZ):
            total += terms[:, j * 2 * C : (j + 1) * 2 * C]
    spectral = total[:, 0:C] + total[:, C:]
    linear = jnp.dot(latent[:, 0:C], skip[...], precision=lax.Precision.HIGHEST, preferred_element_type=F32)
    field = half_gelu(0.5 * (spectral + linear + bias[...]))
    out[...] = jnp.concatenate([field, jnp.zeros_like(field)], axis=1).astype(BF)


def decode_body(
    owner_row, owner_col, returned, proj, w1, w2, b2, w3, centres, fill, offsets, points,
    out, gathered, totals, features, iota,
):
    step = pl.program_id(0)

    @pl.when(step == 0)
    def _():
        before = lax.broadcasted_iota(jnp.int32, (BLKS, BLKS), 1) < lax.broadcasted_iota(
            jnp.int32, (BLKS, BLKS), 0
        )
        same = owner_col[...] == owner_row[...]
        rank = jnp.sum(jnp.where(same & before, 1, 0), axis=1, keepdims=True)
        target = owner_col[...] * SLOTS + rank
        slot = lax.broadcasted_iota(jnp.int32, (BLKS, ENTRIES), 1)
        picker = jnp.where(slot == target, 1.0, 0.0).astype(BF)
        values = dot(picker, returned[...]).astype(BF)
        gathered[...] = dot(values[:, 0:C], proj[...], NT)
        fill_iota(iota)
        totals[...] = jnp.zeros_like(totals)

    distance = block_lanes()
    live = jnp.where((distance >= 0) & (distance < fill[...]), 1.0, 0.0)
    alive = jnp.sum(live, axis=0, keepdims=True)
    live = live.astype(BF)
    inputs = edge_features(offsets, centres, distance, features)
    rows = pl.ds(pl.multiple_of(step * STEP_BLKS, STEP_BLKS), STEP_BLKS)
    cells = gathered[rows, :]
    cells_high = cells.astype(BF)
    cells_low = (cells - cells_high.astype(F32)).astype(BF)
    pieces = jnp.concatenate([cells_high, cells_low], axis=0)
    live = jnp.concatenate([live, live], axis=0)
    for sub in range(LANES // SUB):
        lanes = slice(sub * SUB, (sub + 1) * SUB)
        weight = network(w1[...], w2[...], b2[...], w3[...], inputs[:, lanes])
        message = (weight * dot(pieces, live[:, lanes], TN)).astype(BF)
        row = point_rows(points, sub)
        high = jnp.broadcast_to((row >> 8).astype(F32), (16, SUB)).astype(BF)
        high_rows = jnp.concatenate([high] * (C // 16), axis=0)
        parts = [
            jnp.where(high_rows == jnp.full((), i, BF), message, jnp.zeros((), BF)) for i in range(HIGH)
        ]
        number = lax.broadcasted_iota(jnp.int32, (16, SUB), 0)
        count = jnp.where(number == row >> 8, jnp.broadcast_to(alive[:, lanes], (16, SUB)), 0.0)
        parts.append(count.astype(BF))
        totals[...] += dot(jnp.concatenate(parts, axis=0), low_onehot(row, iota), NT)

    @pl.when(step == BLKS // STEP_BLKS - 1)
    def _():
        for high in range(HIGH):
            degree = totals[HIGH * C + high : HIGH * C + high + 1, :]
            scale = 1.0 / jnp.maximum(jnp.sqrt(degree), 1.0)
            value = totals[high * C : (high + 1) * C, :] * scale
            out[:, high * LOW : (high + 1) * LOW] = value.astype(BF)


def whole(shape):
    return pl.BlockSpec(shape, lambda i: (0,) * len(shape))


def edge_specs():
    return [
        whole((H, 16)),
        whole((H, H)),
        whole((H, ROWS)),
        whole((C, H)),
        pl.BlockSpec((1, 16, STEP_BLKS), lambda i: (i, 0, 0)),
        pl.BlockSpec((STEP_BLKS, 1), lambda i: (i, 0)),
        pl.BlockSpec((3, LANES), lambda i: (0, i)),
        pl.BlockSpec((STEP_BLKS, ROWS), lambda i: (i, 0)),
    ]


PARAMS = pltpu.CompilerParams(vmem_limit_bytes=40 * 1024 * 1024)


def call(body, shapes, scratch=()):
    return pl.pallas_call(
        body,
        out_shape=[jax.ShapeDtypeStruct(shape, kind) for shape, kind in shapes],
        scratch_shapes=list(scratch),
        compiler_params=PARAMS,
        name=body.__name__,
    )


def network_weights(in_w, in_b, mid_w, mid_b, out_w):
    half_b = 0.5 * in_b
    high = half_b.astype(BF)
    low = (half_b - high.astype(F32)).astype(BF)
    first = jnp.concatenate(
        [0.5 * in_w, high[:, None], low[:, None], jnp.zeros((H, 8), BF)], axis=1
    ).astype(BF)
    second_b = jnp.broadcast_to(0.5 * mid_b[:, None], (H, ROWS))
    return first, (0.5 * mid_w).astype(BF), second_b, out_w


def shards(
    point_feats,
    edge_offset,
    edge_point,
    block_fill,
    block_owner,
    block_cell,
    enc_in_w,
    enc_in_b,
    enc_mid_w,
    enc_mid_b,
    enc_out_w,
    point_proj,
    dec_in_w,
    dec_in_b,
    dec_mid_w,
    dec_mid_b,
    dec_out_w,
    cell_proj,
    skip_weight,
    skip_bias,
    spectral_weight,
):
    narrow_here = lax.axis_index("narrow")
    owners = block_owner[:, 0]
    coord_x = owners * XL + block_cell // (YL * G)
    coord_y = narrow_here * YL + block_cell // G % YL
    coord_z = block_cell % G
    coords = jnp.stack([coord_x, coord_y, coord_z], axis=0).astype(F32)
    centres = ((2.0 * coords + 1.0) / G - 1.0).astype(BF)
    steps = BLKS // STEP_BLKS
    tall = jnp.concatenate(
        [jnp.zeros((3, BLKS), BF), centres, jnp.ones((2, BLKS), BF), jnp.zeros((8, BLKS), BF)], axis=0
    )
    tall = tall.reshape(16, steps, STEP_BLKS).transpose(1, 0, 2)
    owner_row = owners[None, :]
    fill_col = block_fill[:, None]
    facts = jnp.stack([block_cell // G, coord_z, block_fill], axis=1).astype(F32)
    meta = jnp.pad(facts, ((0, 0), (C, C - 3)))

    scratch = [pltpu.VMEM((16, LANES), F32), pltpu.VMEM((LOW, SUB), BF)]
    arbitrary = pltpu.CompilerParams(
        vmem_limit_bytes=40 * 1024 * 1024, dimension_semantics=("arbitrary",)
    )
    sent = pl.pallas_call(
        encode_body,
        grid=(steps,),
        out_shape=jax.ShapeDtypeStruct((ENTRIES, 2 * C), BF),
        in_specs=[
            whole((1, BLKS)),
            whole((BLKS, 1)),
            whole((BLKS, 2 * C)),
            whole((C, PTS)),
            whole((C, C)),
        ]
        + edge_specs(),
        out_specs=whole((ENTRIES, 2 * C)),
        scratch_shapes=[pltpu.VMEM((HIGH * C, LOW), BF), pltpu.VMEM((BLKS, 2 * C), F32)] + scratch,
        compiler_params=arbitrary,
        name="encode",
    )(
        owner_row,
        block_owner,
        meta,
        point_feats,
        point_proj,
        *network_weights(enc_in_w, enc_in_b, enc_mid_w, enc_mid_b, enc_out_w),
        tall,
        fill_col,
        edge_offset,
        edge_point,
    )

    def swap(value, axis, count):
        value = value.reshape(count, value.size // count // value.shape[-1], value.shape[-1])
        return lax.all_to_all(value, axis, split_axis=0, concat_axis=0, tiled=True)

    table_z = jnp.asarray(z_table())
    received = swap(sent, "wide", WIDE).reshape(ENTRIES, 2 * C)
    pencils, latent = call(
        forward_z_body, [((NARROW, YL, XL * KZ * 2 * C), BF), ((ENTRIES, 2 * C), F32)]
    )(received, table_z)
    columns = swap(pencils, "narrow", NARROW).reshape(G, XL * KZ * 2 * C)
    work = pltpu.VMEM((M * XL * KZ, 2 * C), F32)
    (y_modes,) = call(forward_y_body, [((M * XL * KZ, 2 * C), BF)], [work])(
        columns, jnp.asarray(y_forward_table())
    )
    slabs = swap(y_modes, "wide", WIDE).reshape(G * KZ, 2 * C)
    (mixed,) = call(
        x_body,
        [((G * KZ, 2 * C), BF)],
        [pltpu.VMEM((M * 2 * KZ, KZ * C), F32), pltpu.VMEM((M * 2 * KZ, 2 * C), F32)],
    )(slabs, jnp.asarray(x_forward_table()), jnp.asarray(x_inverse_table()), spectral_weight[0])
    rows = swap(mixed, "wide", WIDE).reshape(M * XL * KZ, 2 * C)
    (grid_modes,) = call(inverse_y_body, [((G, XL * KZ * 2 * C), BF)], [work])(
        rows, jnp.asarray(y_inverse_table())
    )
    spectra = swap(grid_modes, "narrow", NARROW)
    (reply,) = call(inverse_z_body, [((ENTRIES, 2 * C), BF)])(
        received, latent, spectra, table_z, skip_weight, skip_bias[None, :]
    )
    returned = swap(reply, "wide", WIDE).reshape(ENTRIES, 2 * C)
    return pl.pallas_call(
        decode_body,
        grid=(steps,),
        out_shape=jax.ShapeDtypeStruct((C, PTS), BF),
        in_specs=[whole((1, BLKS)), whole((BLKS, 1)), whole((ENTRIES, 2 * C)), whole((C, C))]
        + edge_specs(),
        out_specs=whole((C, PTS)),
        scratch_shapes=[pltpu.VMEM((BLKS, C), F32), pltpu.VMEM((HIGH * C + 16, LOW), F32)] + scratch,
        compiler_params=arbitrary,
        name="decode",
    )(
        owner_row,
        block_owner,
        returned,
        cell_proj,
        *network_weights(dec_in_w, dec_in_b, dec_mid_w, dec_mid_b, dec_out_w),
        tall,
        fill_col,
        edge_offset,
        edge_point,
    )


def solution(mesh):
    return jax.shard_map(
        shards,
        mesh=mesh,
        in_specs=(
            P(None, ("wide", "narrow")),
            P(None, ("wide", "narrow")),
            P(("wide", "narrow"), None),
            P(("wide", "narrow")),
            P(("wide", "narrow"), None),
            P(("wide", "narrow")),
            P(),
            P(),
            P(),
            P(),
            P(),
            P(),
            P(),
            P(),
            P(),
            P(),
            P(),
            P(),
            P(),
            P(),
            P("wide", None, "narrow", None, None),
        ),
        out_specs=P(None, ("wide", "narrow")),
        check_vma=False,
    )
```

time: 1030 us -> 224 us (0.22)
  other arithmetic: 378 us -> 5.1 us
  waiting for transfers between devices: 310 us -> 8.98 us
  local copies, waits for them, and re-layouts: 153 us -> 11.2 us
  Pallas kernels: 0 us -> 116 us
  matrix products: 107 us -> 0 us
  blocking collectives: 0 us -> 77.1 us
  starting transfers between devices: 57.2 us -> 3.86 us
  between operations: 14.5 us -> 0.25 us
    scatter-add x4 -> x0, other arithmetic: 355 us -> none  [the longest x1 174 us: shards(): jnp.zeros((chans, point_count), jnp.float32).at[:, flat_points]]
    reduce_scatter x1 -> x0, waiting for transfers between devices: 206 us -> none  [shards(): lax.psum_scatter(jnp.concatenate([real_out, imag_out], axis=3), 'wide', s...]
    gather x4 -> x0, local copies, waits for them, and re-layouts: 125 us -> none  [the longest x2 123 us: shards(): picked = jnp.take(projected, flat_points, axis=1).astype(jnp.float32)]
    pallas_call x0 -> x7, Pallas kernels: none -> 116 us  [the longest x1 59.8 us: shards(): pl.pallas_call(decode_body, grid=(steps,), out_shape=jax.ShapeDtypeStruct...]
    dot_general x32 -> x0, matrix products: 107 us -> none  [the longest x23 54.2 us: einsum_high(): return jnp.einsum(form, left, right, precision=highest)]
    all_gather x1 -> x0, waiting for transfers between devices: 77.7 us -> none  [shards(): piece = lax.all_gather(mixed_modes, 'wide', axis=0, tiled=True)]
    all_to_all x0 -> x5, blocking collectives: none -> 77.1 us  [swap(): return lax.all_to_all(value, axis, split_axis=0, concat_axis=0, tiled=True)]
    all_to_all x6 -> x1, starting transfers between devices: 47.8 us -> 3.86 us  [swap(): return lax.all_to_all(value, axis, split_axis=0, concat_axis=0, tiled=True)]
  transfers between devices with their start and end apart: 8 -> 1, of which waited for: 6 -> 1; matrix products, arithmetic and copies ran while one was open for 34% -> 0% of each run, Pallas kernels for 0% -> 0%
where the time goes in v1:
time: 224 us; the launch traced here: 223 us
  Pallas kernels  116 us (52%)
  blocking collectives  77.1 us (34%)
  local copies, waits for them, and re-layouts  11.2 us (5%)
  waiting for transfers between devices  8.98 us (4%)
  other arithmetic  5.1 us (2%)
  starting transfers between devices  3.86 us (2%)
    all_to_all x5, blocking collectives, swap(): return lax.all_to_all(value, axis, split_axis=0, concat_axis=0, tiled=True)  77.1 us
    pallas_call x1, Pallas kernels, shards(): pl.pallas_call(decode_body, grid=(steps,), out_shape=jax.ShapeDtypeStruct...  59.8 us
    pallas_call x1, Pallas kernels, shards(): pl.pallas_call(encode_body, grid=(steps,), out_shape=jax.ShapeDtypeStruct...  47.8 us
    unnamed x45, local copies, waits for them, and re-layouts  9.38 us
    all_to_all x1, waiting for transfers between devices, swap(): return lax.all_to_all(value, axis, split_axis=0, concat_axis=0, tiled=True)  8.98 us
  transfers between devices with their start and end apart: 1, of which 1 were waited for; matrix products, arithmetic and copies ran while one was open for 0% of the time, Pallas kernels for 0%

profile of v1, /device:TPU:1, one launch (start us, length us, event | category | flops | bytes accessed | tf_op | source)
XLA Modules:
  0.0 222.7 jit_solution(7161444827036391676)
XLA Ops:
  0.0 0.9 copy.64.owner_col
  0.9 0.7 broadcast_multiply_fusion.4
  1.6 0.7 fusion.6
  2.3 0.1 stack.30
  2.4 0.8 copy.63.fill
  3.2 0.7 add_convert_fusion.1
  3.9 0.1 copy.59
  4.0 0.7 convert_bitcast_fusion.1
  4.7 0.7 broadcast_multiply_fusion.2
  5.4 0.1 pad.19.clone
  5.5 0.1 maximum_maximum_fusion.1
  5.6 0.1 copy.62.w1
  5.7 0.8 broadcast_multiply_fusion.1.w2
  6.5 0.7 broadcast_multiply_fusion.6
  7.1 0.1 stack.29
  7.2 0.1 stack.28
  7.3 0.1 pad.11.clone
  7.4 0.1 pad.4.meta
  7.5 0.1 maximum_bitcast_fusion.centres
  7.6 0.1 broadcast_in_dim.39.b2
  7.7 1.0 copy-done.3
  8.8 0.9 copy-done.5
  9.7 0.9 copy-done.9
  10.6 0.7 copy-done.12
  11.3 0.7 copy-done.13
  12.0 0.7 copy-done.17
  12.7 47.8 %encode.1 = bf16[512,128]{1,0:T(8,128)(2,1)S(1)} custom-call(s32[1,256]{1,0:T(1,128)S(1)} %bitcast.38, s32[256,1]{1,0:T(8,128)S(1)} %copy.64.owner_col, f32[256,128]{1,0:T(8,128)S(1)} %pad.4.meta, bf16[64,2048]{1,0:T(8,128)(2,1)S(1)} %copy-done.9, bf16[64,64]{1,0:T(8,128)(2,1)S(1)} %copy-done.12, bf16[128,16]{1,0:T(8,128)(2,1)S(1)} %copy.62.w1, ...), custom_call_target="tpu_custom_call" | custom-call | tf_op jit(solution)/shard_map/encode/pallas_call | solution.py:413
  60.5 21.0 %all_to_all.30 = bf16[32,16,128]{2,1,0:T(8,128)(2,1)S(1)} all-to-all(bf16[32,16,128]{2,1,0:T(8,128)(2,1)S(1)} %bitcast.32), channel_id=1, replica_groups=mesh['wide'=32,'narrow'=8] {'wide'}, dimensions={0} | all-to-all | bytes 262144 | tf_op jit(solution)/shard_map/all_to_all | solution.py:444
  81.5 1.2 copy-done
  82.7 3.0 %forward_z_body.1 = (bf16[8,16,2048]{2,1,0:T(8,128)(2,1)S(1)}, f32[512,128]{1,0:T(8,128)S(1)}) custom-call(bf16[512,128]{1,0:T(8,128)(2,1)S(1)} %bitcast.30, bf16[128,4096]{1,0:T(8,128)(2,1)S(1)} %copy-done), custom_call_target="tpu_custom_call" | custom-call | tf_op jit(solution)/shard_map/forward_z_body/pallas_call | solution.py:448
  85.7 0.0 copy-start.11
  85.7 15.5 %all_to_all.31 = bf16[8,16,2048]{2,1,0:T(8,128)(2,1)S(1)} all-to-all(bf16[8,16,2048]{2,1,0:T(8,128)(2,1)S(1)} %get-tuple-element.8), channel_id=1, replica_groups=mesh['wide'=32,'narrow'=8] {'narrow'}, dimensions={0} | all-to-all | bytes 1048576 | tf_op jit(solution)/shard_map/all_to_all | solution.py:444
  101.2 0.3 forward_y_body.1
  101.6 12.5 %all_to_all.32 = bf16[32,16,128]{2,1,0:T(8,128)(2,1)S(1)} all-to-all(bf16[32,16,128]{2,1,0:T(8,128)(2,1)S(1)} %bitcast.35), channel_id=1, replica_groups=mesh['wide'=32,'narrow'=8] {'wide'}, dimensions={0} | all-to-all | bytes 262144 | tf_op jit(solution)/shard_map/all_to_all | solution.py:444
  114.1 2.2 copy-done.2
  116.3 0.0 copy-start.14
  116.3 0.0 copy-start.15
  116.3 0.0 copy-start.18
  116.3 1.3 x_body.1
  117.6 12.7 %all_to_all.33 = bf16[32,16,128]{2,1,0:T(8,128)(2,1)S(1)} all-to-all(bf16[32,16,128]{2,1,0:T(8,128)(2,1)S(1)} %bitcast.34), channel_id=1, replica_groups=mesh['wide'=32,'narrow'=8] {'wide'}, dimensions={0} | all-to-all | bytes 262144 | tf_op jit(solution)/shard_map/all_to_all | solution.py:444
  130.4 0.5 inverse_y_body.1
  130.9 15.5 %all_to_all.34.spectra = bf16[8,16,2048]{2,1,0:T(8,128)(2,1)S(1)} all-to-all(bf16[8,16,2048]{2,1,0:T(8,128)(2,1)S(1)} %bitcast.29), channel_id=1, replica_groups=mesh['wide'=32,'narrow'=8] {'narrow'}, dimensions={0} | all-to-all | bytes 1048576 | tf_op jit(solution)/shard_map/all_to_all | solution.py:444
  146.4 3.4 %inverse_z_body.1 = bf16[512,128]{1,0:T(8,128)(2,1)} custom-call(bf16[512,128]{1,0:T(8,128)(2,1)S(1)} %bitcast.31, f32[512,128]{1,0:T(8,128)S(1)} %get-tuple-element.7.latent, bf16[8,16,2048]{2,1,0:T(8,128)(2,1)S(1)} %all_to_all.34.spectra, bf16[128,4096]{1,0:T(8,128)(2,1)S(1)} %copy-done.1, f32[64,64]{1,0:T(8,128)S(1)} %copy-done.11, f32[1,64]{1,0:T(1,128)S(1)} %bitcast.40), custom_call_target="tpu_custom_call" | custom-call | tf_op jit(solution)/shard_map/inverse_z_body/pallas_call | solution.py:467
  149.7 3.9 %all-to-all-start.5 = ((bf16[32,16,128]{2,1,0:T(8,128)(2,1)}), bf16[32,16,128]{2,1,0:T(8,128)(2,1)S(1)}, u32[]{:S(2)}, u32[]{:S(2)}) async-start(bf16[32,16,128]{2,1,0:T(8,128)(2,1)} %bitcast.18), calls=%async_computation.5 | async-start | bytes 262144 | tf_op jit(solution)/shard_map/all_to_all | solution.py:444
  153.6 0.1 copy.65.w1
  153.8 9.0 %all-to-all-done.5 = bf16[32,16,128]{2,1,0:T(8,128)(2,1)S(1)} async-done(((bf16[32,16,128]{2,1,0:T(8,128)(2,1)}), bf16[32,16,128]{2,1,0:T(8,128)(2,1)S(1)}, u32[]{:S(2)}, u32[]{:S(2)}) %all-to-all-start.5) | async-done | bytes 131104 | tf_op jit(solution)/shard_map/all_to_all | solution.py:444
  162.7 0.1 broadcast_in_dim.46.b2
  162.9 59.8 %decode.1 = bf16[64,2048]{1,0:T(8,128)(2,1)} custom-call(s32[1,256]{1,0:T(1,128)S(1)} %bitcast.39, s32[256,1]{1,0:T(8,128)S(1)} %copy.64.owner_col, bf16[512,128]{1,0:T(8,128)(2,1)S(1)} %bitcast.37, bf16[64,64]{1,0:T(8,128)(2,1)S(1)} %copy-done.14, bf16[128,16]{1,0:T(8,128)(2,1)S(1)} %copy.65.w1, bf16[128,128]{1,0:T(8,128)(2,1)S(1)} %broadcast_multiply_fusion.w2, ...), custom_call_target="tpu_custom_call" | custom-call | tf_op jit(solution)/shard_map/decode/pallas_call | solution.py:471
  (40 shorter events, 0.1 us)
Async XLA Ops:
  0.0 101.2 %copy-start.16 = (bf16[64,128]{1,0:T(8,128)(2,1)S(1)}, bf16[64,128]{1,0:T(8,128)(2,1)}, u32[]{:S(2)}) copy-start(bf16[64,128]{1,0:T(8,128)(2,1)} %constant.93.clone.table) | copy-start | bytes 49156
  0.0 114.1 %copy-start.7 = (bf16[512,512]{1,0:T(8,128)(2,1)S(1)}, bf16[512,512]{1,0:T(8,128)(2,1)}, u32[]{:S(2)}) copy-start(bf16[512,512]{1,0:T(8,128)(2,1)} %constant.94.clone.forward) | copy-start | bytes 1572868
  0.0 114.1 %copy-start.8 = (bf16[1024,256]{1,0:T(8,128)(2,1)S(1)}, bf16[1024,256]{1,0:T(8,128)(2,1)}, u32[]{:S(2)}) copy-start(bf16[1024,256]{1,0:T(8,128)(2,1)} %constant.95.clone.inverse) | copy-start | bytes 1572868
  7.7 1.1 copy-start.3
  8.8 0.9 copy-start.5
  9.7 0.9 copy-start.9
  10.6 0.7 copy-start.12
  11.3 0.7 copy-start.13
  12.0 0.7 copy-start.17
  81.5 1.2 copy-start
  82.7 47.7 %copy-start.10 = (bf16[256,32]{1,0:T(8,128)(2,1)S(1)}, bf16[256,32]{1,0:T(8,128)(2,1)}, u32[]{:S(2)}) copy-start(bf16[256,32]{1,0:T(8,128)(2,1)} %constant.96.clone.table) | copy-start | bytes 49156
  85.7 60.6 %copy-start.11 = (f32[64,64]{1,0:T(8,128)S(1)}, f32[64,64]{1,0:T(8,128)}, u32[]{:S(2)}) copy-start(f32[64,64]{1,0:T(8,128)} %skip.1) | copy-start | bytes 49156
  101.2 45.1 %copy-start.19 = (f32[64]{0:T(128)S(1)}, f32[64]{0:T(128)}, u32[]{:S(2)}) copy-start(f32[64]{0:T(128)} %param.45) | copy-start | bytes 772
  101.2 45.1 %copy-start.1 = (bf16[128,4096]{1,0:T(8,128)(2,1)S(1)}, bf16[128,4096]{1,0:T(8,128)(2,1)}, u32[]{:S(2)}) copy-start(bf16[128,4096]{1,0:T(8,128)(2,1)} %constant.92.clone.table) | copy-start | bytes 3145732
  114.1 2.2 copy-start.2
  116.2 37.4 %copy-start.21 = (f32[128]{0:T(128)S(1)}, f32[128]{0:T(128)}, u32[]{:S(2)}) copy-start(f32[128]{0:T(128)} %param.41) | copy-start | bytes 1540
  116.2 37.5 %copy-start.20 = (bf16[128,128]{1,0:T(8,128)(2,1)S(1)}, bf16[128,128]{1,0:T(8,128)(2,1)}, u32[]{:S(2)}) copy-start(bf16[128,128]{1,0:T(8,128)(2,1)} %param.40) | copy-start | bytes 98308
  116.3 46.6 %copy-start.4 = (f32[3,32768]{1,0:T(4,128)S(1)}, f32[3,32768]{1,0:T(4,128)}, u32[]{:S(2)}) copy-start(f32[3,32768]{1,0:T(4,128)} %offsets.3) | copy-start | bytes 1179652
  116.3 46.6 %copy-start.6 = (s32[256,128]{1,0:T(8,128)S(1)}, s32[256,128]{1,0:T(8,128)}, u32[]{:S(2)}) copy-start(s32[256,128]{1,0:T(8,128)} %points.3) | copy-start | bytes 393220
  116.3 46.6 %copy-start.14 = (bf16[64,64]{1,0:T(8,128)(2,1)S(1)}, bf16[64,64]{1,0:T(8,128)(2,1)}, u32[]{:S(2)}) copy-start(bf16[64,64]{1,0:T(8,128)(2,1)} %proj.3) | copy-start | bytes 24580
  116.3 46.6 %copy-start.15 = (bf16[64,128]{1,0:T(8,128)(2,1)S(1)}, bf16[64,128]{1,0:T(8,128)(2,1)}, u32[]{:S(2)}) copy-start(bf16[64,128]{1,0:T(8,128)(2,1)} %w3.3) | copy-start | bytes 49156
  116.3 46.6 %copy-start.18 = (s32[256,1]{0,1:T(1,128)S(1)}, s32[256,1]{0,1:T(1,128)}, u32[]{:S(2)}) copy-start(s32[256,1]{0,1:T(1,128)} %param.30) | copy-start | bytes 3076
  149.7 13.0 %all-to-all-start.5 = ((bf16[32,16,128]{2,1,0:T(8,128)(2,1)}), bf16[32,16,128]{2,1,0:T(8,128)(2,1)S(1)}, u32[]{:S(2)}, u32[]{:S(2)}) async-start(bf16[32,16,128]{2,1,0:T(8,128)(2,1)} %bitcast.18), calls=%async_computation.5 | async-start | bytes 262144 | tf_op jit(solution)/shard_map/all_to_all | solution.py:444
